TPU v7x, 32 devices: a whole 2x2x4 slice. The times are simulated.
32 devices in a mesh: groups: 2 (over y), row: 4 (over x, core), col: 4 (over z).
Axes of the slice: x: 2, y: 2, z: 4, core: 2. Of those that a mesh axis runs over, the one named last changes fastest.
Arguments:
- adjacency: bfloat16 [8, 4, 32, 128, 128], P(('groups', 'row'), 'col'), parts along dimension 0, may hold values from 0.049804688 to 1
- tile_row: int32 [8, 4, 32], P(('groups', 'row'), 'col'), parts along dimension 0, may hold values from -1 to 7, as said below
- tile_col: int32 [8, 4, 32], P(('groups', 'row'), 'col'), parts along dimension 0, may hold values from -1 to 7, as said below
- seed_node: int32 [512], P('groups'), parts along dimension 0, may hold values from 0 to 4095
- teleport_block: int32 [512], P('groups'), parts along dimension 0, may hold values from 0 to 31
- previous: float32 [8192, 256], P(('groups', 'row', 'col')), parts along dimension 0, may hold values from 0.1 to 10
Outputs:
- rank_field: float32 [8192, 256], P(('groups', 'row', 'col')), parts along dimension 0
There are 2 independent parts, one for each index of `groups`. A program takes and returns all parts, laid end to end along the dimension named above; each array names one. Nothing has to cross between parts.
Inputs may be any that keep to these rules, and one draw needn't show every extreme that they name: On each device the slots with entries >= 0 come first, and tile_row and tile_col are -1 together on the other slots; a device's (tile_row, tile_col) pairs are distinct; in every part exactly one device has all 32 slots used and every other device uses between 5 and 10 of them. `tile_col`: empty exactly where tile_row is empty. In every part, for each index of row, at least one tile column holds no tile on any device with that index of row.
All inputs are finite; a program needn't handle non-finite values.
Results may differ from a plain program's by a relative error of at most 0.0003.
Values may be sent and summed in bfloat16 or wider, within the bound.
A program may use at most 64 MiB of HBM per device.

v0:
```python
import jax
import jax.numpy as jnp
from jax import lax
from jax.sharding import PartitionSpec as P

TILE = 128
ITERS = 3


damping = 0.85
highest = lax.Precision.HIGHEST


def teleport_weights(node_ids, seed_node, teleport_block):
    at_seed = (node_ids[:, None] == seed_node[None, :]).astype(jnp.float32)
    in_block = ((node_ids // TILE)[:, None] == teleport_block[None, :]).astype(jnp.float32)
    return 4.0 * at_seed + 2.0 * in_block


def block_sum(
    tile_stack, row_ids, col_ids, ordering, sorted_keys, rank_panel, first_row, block_rows
):
    slot_total = tile_stack.shape[0]
    tile_edge = tile_stack.shape[1]
    seed_width = rank_panel.shape[2]
    slot_batch = min(8, slot_total)
    first_live = jnp.sum((sorted_keys < first_row).astype(jnp.int32))
    past_live = jnp.sum((sorted_keys < first_row + block_rows).astype(jnp.int32))
    batches = (past_live - first_live + slot_batch - 1) // slot_batch

    def one_batch(batch_index, accumulated):
        for offset in range(slot_batch):
            position = first_live + batch_index * slot_batch + offset
            slot_index = lax.dynamic_index_in_dim(
                ordering, jnp.minimum(position, slot_total - 1), 0, keepdims=False
            )
            is_live = position < past_live
            target_row = lax.dynamic_index_in_dim(row_ids, slot_index, 0, keepdims=False)
            source_col = lax.dynamic_index_in_dim(col_ids, slot_index, 0, keepdims=False)
            target = jnp.clip(target_row - first_row, 0, block_rows - 1)
            source = jnp.maximum(source_col, 0)
            one_tile = lax.dynamic_index_in_dim(tile_stack, slot_index, 0, keepdims=False)
            panel_block = lax.dynamic_index_in_dim(rank_panel, source, 0, keepdims=False)
            product = jnp.dot(one_tile, panel_block, preferred_element_type=jnp.float32)
            current = lax.dynamic_index_in_dim(accumulated, target, 0, keepdims=False)
            updated = current + jnp.where(is_live, product, jnp.zeros_like(product))
            accumulated = lax.dynamic_update_index_in_dim(accumulated, updated, target, 0)
        return accumulated

    start_sum = jnp.zeros((block_rows, tile_edge, seed_width), jnp.float32)
    result = lax.fori_loop(0, batches, one_batch, start_sum)
    return result.reshape(block_rows * tile_edge, seed_width)


def on_device(adjacency, tile_row, tile_col, seed_node, teleport_block, previous):
    tile_stack = adjacency[0, 0]
    row_ids = tile_row[0, 0]
    col_ids = tile_col[0, 0]
    owned_rows, seed_width = previous.shape
    slot_total = tile_stack.shape[0]
    tile_edge = tile_stack.shape[1]
    row_devices = lax.axis_size("row")
    col_devices = lax.axis_size("col")
    tile_rows = owned_rows * row_devices // tile_edge
    tile_cols = owned_rows * col_devices // tile_edge
    sort_keys = jnp.where(row_ids >= 0, row_ids, tile_rows)
    slot_order = jnp.arange(slot_total, dtype=jnp.int32)
    sorted_keys, ordering = lax.sort((sort_keys, slot_order), num_keys=1, is_stable=True)
    col_place = (col_ids[:, None] == jnp.arange(tile_cols, dtype=jnp.int32)[None, :]).astype(
        jnp.float32
    )
    tile_sums = jnp.sum(tile_stack.astype(jnp.float32), axis=1)
    col_sums = jnp.einsum("tj,tb->jb", col_place, tile_sums, precision=highest).reshape(
        tile_cols * tile_edge
    )
    full_divisor = jnp.maximum(lax.psum(col_sums, "col"), 1.0)
    first_node = (lax.axis_index("row") * col_devices + lax.axis_index("col")) * owned_rows
    node_ids = first_node + jnp.arange(owned_rows, dtype=jnp.int32)
    teleport = teleport_weights(node_ids, seed_node, teleport_block)
    rank_field = previous
    for iteration in range(ITERS):
        gathered = lax.all_gather(rank_field, "col", axis=0, tiled=True)
        rank_panel = (gathered / full_divisor[:, None]).astype(jnp.bfloat16)
        rank_panel = rank_panel.reshape(tile_cols, tile_edge, seed_width)
        partial_sum = block_sum(
            tile_stack, row_ids, col_ids, ordering, sorted_keys, rank_panel, 0, tile_rows
        )
        summed = lax.psum_scatter(partial_sum, "row", scatter_dimension=0, tiled=True)
        rank_field = damping * summed + (1.0 - damping) * teleport
    return rank_field


def solution(mesh):
    in_specs = (
        P(("groups", "row"), "col", None, None, None),
        P(("groups", "row"), "col", None),
        P(("groups", "row"), "col", None),
        P("groups"),
        P("groups"),
        P(("groups", "row", "col"), None),
    )
    out_specs = P(("groups", "row", "col"), None)
    return jax.shard_map(
        on_device, mesh=mesh, in_specs=in_specs, out_specs=out_specs, check_vma=False
    )
```

profile of v0, /device:TPU:0, one launch (start us, length us, event | category | flops | bytes accessed | tf_op | source)
XLA Modules:
  0.0 590.4 jit_solution(7642503846385073427)
XLA Ops:
  8.0 1.1 sort.15
  11.1 1.4 convert_reduce_fusion
  12.7 13.6 %psum.7 = f32[1024]{0:T(1024)S(1)} all-reduce(f32[1024]{0:T(1024)S(1)} %convolution_bitcast_fusion), channel_id=1, replica_groups=mesh['groups'=2,'row'=4,'col'=4] {'col'}, use_global_device_ids=true, to_apply=%region_4.5 | all-reduce | flops 1024 | bytes 8192 | tf_op jit(solution)/shard_map/psum | solution.py:76
  26.4 13.3 %all-gather.4.cloned.1.call-done = f32[1024,256]{1,0:T(8,128)} async-done(((f32[256,256]{1,0:T(8,128)}), f32[1024,256]{1,0:T(8,128)}) %all-gather.4.cloned.1.call-update) | async-done | bytes 1048592 | tf_op jit(solution)/shard_map/all_gather | solution.py:82
  39.6 1.4 divide_convert_fusion.2
  41.2 33.7 %while.30 = (s32[]{:T(128)}, f32[8,128,256]{2,1,0:T(8,128)S(1)}, s32[]{:T(128)}, s32[]{:T(128)}, s32[32]{0:T(128)S(1)}, /*index=5*/s32[32]{0:T(128)S(1)}, s32[]{...) while((s32[]{:T(128)}, f32[8,128,256]{2,1,0:T(8,128)S(1)}, ...), condition=%wide.region_6.7_spmd, body=%wide.region_5.6_spmd.sunk | while | flops 67633232 | bytes 4982441 | solution.py:51
  57.6 0.7 fusion.301
  74.9 0.9 copy-done.1
  76.0 124.2 %reduce-scatter.4.cloned.1.call-done = f32[256,256]{1,0:T(8,128)} async-done(((f32[1024,256]{1,0:T(8,128)}), f32[256,256]{1,0:T(8,128)}) %reduce-scatter.4.cloned.1.call-update) | async-done | bytes 262160 | tf_op jit(solution)/shard_map/reduce_scatter | solution.py:88
  200.2 1.8 fusion.192
  202.1 28.1 %all-gather.6.cloned.1.call-done = f32[1024,256]{1,0:T(8,128)} async-done(((f32[256,256]{1,0:T(8,128)}), f32[1024,256]{1,0:T(8,128)}) %all-gather.6.cloned.1.call-update) | async-done | bytes 1048592 | tf_op jit(solution)/shard_map/all_gather | solution.py:82
  230.1 1.4 divide_convert_fusion.1
  231.7 33.8 %while.31 = (s32[]{:T(128)}, f32[8,128,256]{2,1,0:T(8,128)S(1)}, s32[]{:T(128)}, s32[]{:T(128)}, s32[32]{0:T(128)S(1)}, /*index=5*/s32[32]{0:T(128)S(1)}, s32[]{...) while((s32[]{:T(128)}, f32[8,128,256]{2,1,0:T(8,128)S(1)}, ...), condition=%wide.region_9.10_spmd, body=%wide.region_8.9_spmd.sunk | while | flops 67633232 | bytes 4982441 | solution.py:51
  248.2 0.7 fusion.327
  265.5 1.0 copy-done.2
  266.5 124.5 %reduce-scatter.6.cloned.1.call-done = f32[256,256]{1,0:T(8,128)} async-done(((f32[1024,256]{1,0:T(8,128)}), f32[256,256]{1,0:T(8,128)}) %reduce-scatter.6.cloned.1.call-update) | async-done | bytes 262160 | tf_op jit(solution)/shard_map/reduce_scatter | solution.py:88
  391.0 1.8 multiply_add_fusion.1
  392.8 28.0 %all-gather.8.cloned.1.call-done = f32[1024,256]{1,0:T(8,128)} async-done(((f32[256,256]{1,0:T(8,128)}), f32[1024,256]{1,0:T(8,128)}) %all-gather.8.cloned.1.call-update) | async-done | bytes 1048592 | tf_op jit(solution)/shard_map/all_gather | solution.py:82
  420.9 1.4 divide_convert_fusion
  422.4 33.8 %while.32 = (s32[]{:T(128)}, f32[8,128,256]{2,1,0:T(8,128)S(1)}, s32[]{:T(128)}, s32[]{:T(128)}, s32[32]{0:T(128)S(1)}, /*index=5*/s32[32]{0:T(128)S(1)}, s32[]{...) while((s32[]{:T(128)}, f32[8,128,256]{2,1,0:T(8,128)S(1)}, ...), condition=%wide.region_12.13_spmd, body=%wide.region_11.12_spmd.sunk | while | flops 67633232 | bytes 4982441 | solution.py:51
  438.9 0.7 fusion.353
  456.2 1.0 copy-done
  457.2 124.5 %reduce-scatter.8.cloned.1.call-done = f32[256,256]{1,0:T(8,128)} async-done(((f32[1024,256]{1,0:T(8,128)}), f32[256,256]{1,0:T(8,128)}) %reduce-scatter.8.cloned.1.call-update) | async-done | bytes 262160 | tf_op jit(solution)/shard_map/reduce_scatter | solution.py:88
  581.7 1.8 multiply_add_fusion
  (85 shorter events, 9.2 us)
Async XLA Ops:
  6.5 5.9 %copy-start.5 = (s32[1,1,32]{2,1,0:T(1,128)S(1)}, s32[1,1,32]{2,1,0:T(1,128)}, u32[]{:S(2)}) copy-start(s32[1,1,32]{2,1,0:T(1,128)} %param.14) | copy-start | bytes 388
  6.5 33.1 %all-gather.4.cloned.1.call-start = ((), (), s32[]{:S(2)}) async-start(), calls=%async_computation.3 | async-start | bytes 1310720 | tf_op jit(solution)/shard_map/all_gather | solution.py:82
  7.3 192.9 %reduce-scatter.4.cloned.1.call-start = ((), (), s32[]{:S(2)}) async-start(), calls=%async_computation.4 | async-start | bytes 1310720 | tf_op jit(solution)/shard_map/reduce_scatter | solution.py:88
  26.4 14.8 %copy-start.3 = (bf16[1,1,32,128,128]{4,3,2,1,0:T(8,128)(2,1)S(1)}, bf16[1,1,32,128,128]{4,3,2,1,0:T(8,128)(2,1)}, u32[]{:S(2)}) copy-start(bf16[1,1,32,128,128]{4,3,2,1,0:T(8,128)(2,1)} %param.12) | copy-start | bytes 3145732
  26.4 14.8 %copy-start.4 = (s32[1,1,32]{2,1,0:T(1,128)S(1)}, s32[1,1,32]{2,1,0:T(1,128)}, u32[]{:S(2)}) copy-start(s32[1,1,32]{2,1,0:T(1,128)} %param.13) | copy-start | bytes 388
  74.9 1.0 copy-start.1
  74.9 125.3 %copy-start.6 = (s32[256]{0:T(256)S(1)}, s32[256]{0:T(256)}, u32[]{:S(2)}) copy-start(s32[256]{0:T(256)} %param.16) | copy-start | bytes 3076
  74.9 125.3 %copy-start.7 = (s32[256]{0:T(256)S(1)}, s32[256]{0:T(256)}, u32[]{:S(2)}) copy-start(s32[256]{0:T(256)} %param.15) | copy-start | bytes 3076
  75.9 154.2 %all-gather.6.cloned.1.call-start = ((), (), s32[]{:S(2)}) async-start(), calls=%async_computation.5 | async-start | bytes 1310720 | tf_op jit(solution)/shard_map/all_gather | solution.py:82
  202.0 189.0 %reduce-scatter.6.cloned.1.call-start = ((), (), s32[]{:S(2)}) async-start(), calls=%async_computation.6 | async-start | bytes 1310720 | tf_op jit(solution)/shard_map/reduce_scatter | solution.py:88
  265.5 1.0 copy-start.2
  266.5 154.4 %all-gather.8.cloned.1.call-start = ((), (), s32[]{:S(2)}) async-start(), calls=%async_computation.7 | async-start | bytes 1310720 | tf_op jit(solution)/shard_map/all_gather | solution.py:82
  392.8 188.9 %reduce-scatter.8.cloned.1.call-start = ((), (), s32[]{:S(2)}) async-start(), calls=%async_computation.8 | async-start | bytes 1310720 | tf_op jit(solution)/shard_map/reduce_scatter | solution.py:88
  456.2 1.0 copy-start
Sparse Core Ops, SparseCore 0:
  8.9 30.6 all-gather.3
  76.0 124.1 reduce-scatter.3
  202.1 27.9 all-gather.5
  266.6 124.3 reduce-scatter.5
  392.9 27.9 all-gather.7
  457.3 124.3 reduce-scatter.7
where the time goes:
time: 597 us; the launch traced here: 590 us
  waiting for transfers between devices  443 us (74%)
  loops' own time  92.9 us (16%)
  between operations  14.9 us (2%)
  other arithmetic  13.6 us (2%)
  blocking collectives  13.6 us (2%)
  local copies, waits for them, and re-layouts  7.78 us (1%)
    reduce_scatter x3, waiting for transfers between devices, on_device(): lax.psum_scatter(partial_sum, 'row', scatter_dimension=0, tiled=True)  373 us
    another operation x3, loops' own time, block_sum(): result = lax.fori_loop(0, batches, one_batch, start_sum)  92.9 us
    all_gather x3, waiting for transfers between devices, on_device(): gathered = lax.all_gather(rank_field, 'col', axis=0, tiled=True)  69.4 us
    psum x1, blocking collectives, on_device(): full_divisor = jnp.maximum(lax.psum(col_sums, 'col'), 1.0)  13.6 us
  transfers between devices with their start and end apart: 6, of which 6 were waited for; matrix products, arithmetic and copies ran while one was open for 1% of the time, Pallas kernels for 0%

commit v1 on v0

v1 whole, which is shorter than its diff:
```python
import functools

import jax
import jax.numpy as jnp
from jax import lax
from jax.experimental import pallas as pl
from jax.experimental.pallas import tpu as pltpu
from jax.sharding import PartitionSpec as P

ITERS = 3
LANES = 128
DAMPING = 0.85
MESH = pl.DeviceIdType.MESH


def refresh_kernel(
    n_row, n_col, slot_ref, adj_ref, seed_ref, block_ref, prev_ref, out_ref,
    link, sums_out, sums_in, inverse, restart, panels, mine,
    half_out, half_in, full_out, full_in,
    sums_ss, sums_rs, col_ss, col_rs, row_ss, row_rs,
):
    r, c = lax.axis_index("row"), lax.axis_index("col")
    owned, seeds = prev_ref.shape
    edge = adj_ref.shape[1]
    targets, sources = link.shape
    tile_rows, tile_cols = targets // edge, sources // edge
    chunks = seeds // LANES

    barrier = pltpu.get_barrier_semaphore()
    for d in range(1, n_col):
        pl.semaphore_signal(barrier, 1, device_id={"col": lax.rem(c + d, n_col)}, device_id_type=MESH)
    for e in range(1, n_row):
        pl.semaphore_signal(barrier, 1, device_id={"row": lax.rem(r + e, n_row)}, device_id_type=MESH)

    @pl.loop(0, tile_rows)
    def _(i):
        for j in range(tile_cols):
            slot = slot_ref[i * tile_cols + j]
            tile = adj_ref[jnp.maximum(slot - 1, 0)]
            link[pl.ds(i * edge, edge), j * edge : (j + 1) * edge] = jnp.where(
                slot > 0, tile, jnp.zeros_like(tile)
            )

    ones = jnp.ones((16, targets), jnp.bfloat16)
    for k in range(n_col):
        columns = slice(k * owned, (k + 1) * owned)
        total = jnp.dot(ones, link[:, columns], preferred_element_type=jnp.float32)
        sums_out[k] = total[:8]

    pl.semaphore_wait(barrier, n_col - 1 + n_row - 1)

    def sums_copy(d):
        dst = lax.rem(c + d, n_col)
        return pltpu.make_async_remote_copy(
            src_ref=sums_out.at[dst], dst_ref=sums_in.at[d],
            send_sem=sums_ss.at[d], recv_sem=sums_rs.at[d],
            device_id={"col": dst}, device_id_type=MESH,
        )

    def col_copy(it, h, d):
        dst = lax.rem(c + d, n_col)
        place = panels.at[it, h, pl.ds(pl.multiple_of(c * owned, owned), owned)]
        return pltpu.make_async_remote_copy(
            src_ref=place, dst_ref=place,
            send_sem=col_ss.at[it, h, d], recv_sem=col_rs.at[it, h, d],
            device_id={"col": dst}, device_id_type=MESH,
        )

    def row_copy(it, h, e):
        last = it == ITERS - 1
        src = full_out.at[h, e] if last else half_out.at[it, h, e]
        dst = full_in.at[h, e] if last else half_in.at[it, h, e]
        return pltpu.make_async_remote_copy(
            src_ref=src, dst_ref=dst,
            send_sem=row_ss.at[it, h, e], recv_sem=row_rs.at[it, h, e],
            device_id={"row": lax.rem(r + e, n_row)}, device_id_type=MESH,
        )

    for d in range(1, n_col):
        sums_copy(d).start()

    row_of = lax.broadcasted_iota(jnp.int32, (owned, seeds), 0)
    first = (r * n_col + c) * owned
    at_seed = (row_of + first == seed_ref[...]).astype(jnp.float32)
    in_block = ((row_of + first) // edge == block_ref[...]).astype(jnp.float32)
    restart[...] = (1.0 - DAMPING) * (4.0 * at_seed + 2.0 * in_block)

    total = sums_out[c]
    for d in range(1, n_col):
        sums_copy(d).wait_recv()
        total = total + sums_in[d]
    wide = jnp.broadcast_to(1.0 / jnp.maximum(total[0:1], 1.0), (LANES, owned))
    inverse[...] = jnp.transpose(wide)

    def share(it, h, ranks):
        place = pl.ds(pl.multiple_of(c * owned, owned), owned)
        panels[it, h, place] = (ranks * inverse[...]).astype(jnp.bfloat16)
        for d in range(1, n_col):
            col_copy(it, h, d).start()

    for h in range(chunks):
        share(0, h, prev_ref[:, h * LANES : (h + 1) * LANES])

    for it in range(ITERS):
        for h in range(chunks):
            for d in range(1, n_col):
                col_copy(it, h, d).wait_recv()
            for e in list(range(1, n_row)) + [0]:
                dst = lax.rem(r + e, n_row)
                rows = pl.ds(pl.multiple_of(dst * owned, owned), owned)
                part = jnp.dot(link[rows, :], panels[it, h], preferred_element_type=jnp.float32)
                if e == 0:
                    mine[it, h] = part
                else:
                    if it == ITERS - 1:
                        full_out[h, e] = part
                    else:
                        half_out[it, h, e] = part.astype(jnp.bfloat16)
                    row_copy(it, h, e).start()
        for h in range(chunks):
            summed = mine[it, h]
            for e in range(1, n_row):
                row_copy(it, h, e).wait_recv()
                if it == ITERS - 1:
                    summed = summed + full_in[h, e]
                else:
                    summed = summed + half_in[it, h, e].astype(jnp.float32)
            lanes = slice(h * LANES, (h + 1) * LANES)
            ranks = DAMPING * summed + restart[:, lanes]
            if it == ITERS - 1:
                out_ref[:, lanes] = ranks
            else:
                share(it + 1, h, ranks)

    for d in range(1, n_col):
        sums_copy(d).wait_send()
    for it in range(ITERS):
        for h in range(chunks):
            for d in range(1, n_col):
                col_copy(it, h, d).wait_send()
            for e in range(1, n_row):
                row_copy(it, h, e).wait_send()


def on_device(adjacency, tile_row, tile_col, seed_node, teleport_block, previous):
    tiles = adjacency[0, 0]
    rows, cols = tile_row[0, 0], tile_col[0, 0]
    slots, edge = tiles.shape[:2]
    owned, seeds = previous.shape
    n_row, n_col = lax.axis_size("row"), lax.axis_size("col")
    targets, sources = n_row * owned, n_col * owned
    tile_rows, tile_cols = targets // edge, sources // edge
    chunks = seeds // LANES
    key = jnp.where(rows >= 0, rows * tile_cols + cols, -1)
    places = jnp.arange(tile_rows * tile_cols, dtype=jnp.int32)
    number = jnp.arange(1, slots + 1, dtype=jnp.int32)
    slot_of = jnp.sum(jnp.where(places[:, None] == key[None, :], number[None, :], 0), axis=1)
    vmem = pl.BlockSpec(memory_space=pltpu.VMEM)
    dma = pltpu.SemaphoreType.DMA
    return pl.pallas_call(
        functools.partial(refresh_kernel, n_row, n_col),
        out_shape=jax.ShapeDtypeStruct((owned, seeds), jnp.float32),
        in_specs=[pl.BlockSpec(memory_space=pltpu.SMEM)] + [vmem] * 4,
        out_specs=vmem,
        scratch_shapes=[
            pltpu.VMEM((targets, sources), jnp.bfloat16),
            pltpu.VMEM((n_col, 8, owned), jnp.float32),
            pltpu.VMEM((n_col, 8, owned), jnp.float32),
            pltpu.VMEM((owned, LANES), jnp.float32),
            pltpu.VMEM((owned, seeds), jnp.float32),
            pltpu.VMEM((ITERS, chunks, sources, LANES), jnp.bfloat16),
            pltpu.VMEM((ITERS, chunks, owned, LANES), jnp.float32),
            pltpu.VMEM((ITERS - 1, chunks, n_row, owned, LANES), jnp.bfloat16),
            pltpu.VMEM((ITERS - 1, chunks, n_row, owned, LANES), jnp.bfloat16),
            pltpu.VMEM((chunks, n_row, owned, LANES), jnp.float32),
            pltpu.VMEM((chunks, n_row, owned, LANES), jnp.float32),
            dma((n_col,)),
            dma((n_col,)),
            dma((ITERS, chunks, n_col)),
            dma((ITERS, chunks, n_col)),
            dma((ITERS, chunks, n_row)),
            dma((ITERS, chunks, n_row)),
        ],
        compiler_params=pltpu.CompilerParams(
            collective_id=0, has_side_effects=True, vmem_limit_bytes=56 * 2**20
        ),
    )(slot_of, tiles, seed_node[None, :], teleport_block[None, :], previous)


def solution(mesh):
    in_specs = (
        P(("groups", "row"), "col", None, None, None),
        P(("groups", "row"), "col", None),
        P(("groups", "row"), "col", None),
        P("groups"),
        P("groups"),
        P(("groups", "row", "col"), None),
    )
    out_specs = P(("groups", "row", "col"), None)
    return jax.shard_map(
        on_device, mesh=mesh, in_specs=in_specs, out_specs=out_specs, check_vma=False
    )
```

time: 597 us -> 62.4 us (0.10)
  waiting for transfers between devices: 443 us -> 0 us
  loops' own time: 92.9 us -> 0 us
  Pallas kernels: 0 us -> 58.3 us
  between operations: 14.9 us -> 0.01 us
  blocking collectives: 13.6 us -> 0 us
  other arithmetic: 13.6 us -> 0.61 us
    reduce_scatter x3 -> x0, waiting for transfers between devices: 373 us -> none  [on_device(): lax.psum_scatter(partial_sum, 'row', scatter_dimension=0, tiled=True)]
    another operation x3 -> x0, loops' own time: 92.9 us -> none  [block_sum(): result = lax.fori_loop(0, batches, one_batch, start_sum)]
    all_gather x3 -> x0, waiting for transfers between devices: 69.4 us -> none  [on_device(): gathered = lax.all_gather(rank_field, 'col', axis=0, tiled=True)]
    pallas_call x0 -> x1, Pallas kernels: none -> 58.3 us  [on_device(): pl.pallas_call(functools.partial(refresh_kernel, n_row, n_col), out_shape...]
    psum x1 -> x0, blocking collectives: 13.6 us -> none  [on_device(): full_divisor = jnp.maximum(lax.psum(col_sums, 'col'), 1.0)]
  transfers between devices with their start and end apart: 6 -> 0, of which waited for: 6 -> 0; matrix products, arithmetic and copies ran while one was open for 1% -> 0% of each run, Pallas kernels for 0% -> 0%
where the time goes in v1:
time: 62.4 us; the launch traced here: 61.2 us
  Pallas kernels  58.3 us (93%)
  local copies, waits for them, and re-layouts  2.34 us (4%)
    pallas_call x1, Pallas kernels, on_device(): pl.pallas_call(functools.partial(refresh_kernel, n_row, n_col), out_shape...  58.3 us
    unnamed x5, local copies, waits for them, and re-layouts  2.34 us

profile of v1, /device:TPU:0, one launch (start us, length us, event | category | flops | bytes accessed | tf_op | source)
XLA Modules:
  0.0 61.2 jit_solution(6260004764303747044)
XLA Ops:
  0.0 0.0 copy-start
  0.0 0.0 copy-start.1
  0.0 0.7 %copy-done = s32[1,1,32]{2,1,0:T(1,128)S(1)} copy-done((s32[1,1,32]{2,1,0:T(1,128)S(1)}, s32[1,1,32]{2,1,0:T(1,128)}, u32[]{:S(2)}) %copy-start) | copy-done | bytes 152
  0.7 0.0 copy-done.1
  0.7 0.6 select_reduce_fusion.slot_ref
  1.3 58.3 %shard_map.64 = f32[256,256]{1,0:T(8,128)} custom-call(s32[64]{0:T(128)} %select_reduce_fusion.slot_ref, bf16[32,128,128]{2,1,0:T(8,128)(2,1)} %bitcast.5, s32[1,256]{1,0:T(1,128)} %bitcast.6, s32[1,256]{1,0:T(1,128)} %bitcast.7, f32[256,256]{1,0:T(8,128)} %prev_ref.1), custom_call_target="tpu_custom_call" | custom-call | tf_op jit(solution)/shard_map/pallas_call | solution.py:160
  59.6 1.7 %copy.8 = f32[256,256]{1,0:T(8,128)} copy(f32[256,256]{1,0:T(8,128)} %shard_map.64) | data formatting | bytes 524288
  (2 shorter events, 0.0 us)
Async XLA Ops:
  0.0 0.7 %copy-start = (s32[1,1,32]{2,1,0:T(1,128)S(1)}, s32[1,1,32]{2,1,0:T(1,128)}, u32[]{:S(2)}) copy-start(s32[1,1,32]{2,1,0:T(1,128)} %param.7) | copy-start | bytes 388
  0.0 0.7 %copy-start.1 = (s32[1,1,32]{2,1,0:T(1,128)S(1)}, s32[1,1,32]{2,1,0:T(1,128)}, u32[]{:S(2)}) copy-start(s32[1,1,32]{2,1,0:T(1,128)} %param.8) | copy-start | bytes 388

commit v2 on v1

v2 whole, which is shorter than its diff:
```python
import functools

import jax
import jax.numpy as jnp
from jax import lax
from jax.experimental import pallas as pl
from jax.experimental.pallas import tpu as pltpu
from jax.sharding import PartitionSpec as P

ITERS = 3
LANES = 128
DAMPING = 0.85
MESH = pl.DeviceIdType.MESH


def refresh_kernel(
    n_row, n_col, slot_ref, tiles_ref, tile_col_ref, seed_ref, block_ref, prev_ref, out_ref,
    adj_ref, adj_sem, link, sums_out, sums_in, inverse, restart, panels, kept,
    pair_out, pair_in, half_out, half_in, full_out, full_in,
    sums_ss, sums_rs, col_ss, col_rs, pair_ss, pair_rs, row_ss, row_rs,
):
    r, c = lax.axis_index("row"), lax.axis_index("col")
    owned, seeds = prev_ref.shape
    slots, edge = adj_ref.shape[:2]
    held = owned // edge
    targets, sources = link.shape
    tile_rows, tile_cols = targets // edge, sources // edge
    chunks = seeds // LANES
    chips = n_row // 2
    chip, core = r // 2, lax.rem(r, 2)
    mate = r + 1 - 2 * core

    barrier = pltpu.get_barrier_semaphore()
    for d in range(1, n_col):
        pl.semaphore_signal(barrier, 1, device_id={"col": lax.rem(c + d, n_col)}, device_id_type=MESH)
    pl.semaphore_signal(barrier, 1, device_id={"row": mate}, device_id_type=MESH)
    for e in range(1, chips):
        pl.semaphore_signal(
            barrier, 1, device_id={"row": lax.rem(chip + e, chips) * 2 + core}, device_id_type=MESH
        )

    load = pltpu.make_async_copy(tiles_ref, adj_ref, adj_sem)
    load.start()
    row_of = lax.broadcasted_iota(jnp.int32, (owned, seeds), 0)
    first = (r * n_col + c) * owned
    at_seed = (row_of + first == seed_ref[...]).astype(jnp.float32)
    in_block = ((row_of + first) // edge == block_ref[...]).astype(jnp.float32)
    restart[...] = (1.0 - DAMPING) * (4.0 * at_seed + 2.0 * in_block)
    load.wait()

    tile_sums = jnp.sum(adj_ref[...].astype(jnp.float32), axis=1)
    column_of = lax.broadcasted_iota(jnp.int32, (tile_cols, slots), 0)
    placed = (column_of == tile_col_ref[...]).astype(jnp.float32)
    sums = jnp.dot(
        placed, tile_sums, precision=lax.Precision.HIGHEST, preferred_element_type=jnp.float32
    )
    for k in range(n_col):
        sums_out[k, :held] = sums[k * held : (k + 1) * held]

    pl.semaphore_wait(barrier, n_col - 1 + chips)

    def sums_copy(d):
        dst = lax.rem(c + d, n_col)
        return pltpu.make_async_remote_copy(
            src_ref=sums_out.at[dst], dst_ref=sums_in.at[d],
            send_sem=sums_ss.at[d], recv_sem=sums_rs.at[d],
            device_id={"col": dst}, device_id_type=MESH,
        )

    def col_copy(it, h, d):
        dst = lax.rem(c + d, n_col)
        place = panels.at[it, h, pl.ds(pl.multiple_of(c * owned, owned), owned)]
        return pltpu.make_async_remote_copy(
            src_ref=place, dst_ref=place,
            send_sem=col_ss.at[it, h, d], recv_sem=col_rs.at[it, h, d],
            device_id={"col": dst}, device_id_type=MESH,
        )

    def pair_copy(it, h, e):
        return pltpu.make_async_remote_copy(
            src_ref=pair_out.at[it, h, e], dst_ref=pair_in.at[it, h, e],
            send_sem=pair_ss.at[it, h, e], recv_sem=pair_rs.at[it, h, e],
            device_id={"row": mate}, device_id_type=MESH,
        )

    def row_copy(it, h, e):
        last = it == ITERS - 1
        src = full_out.at[h, e] if last else half_out.at[it, h, e]
        dst = full_in.at[h, e] if last else half_in.at[it, h, e]
        return pltpu.make_async_remote_copy(
            src_ref=src, dst_ref=dst,
            send_sem=row_ss.at[it, h, e], recv_sem=row_rs.at[it, h, e],
            device_id={"row": lax.rem(chip + e, chips) * 2 + core}, device_id_type=MESH,
        )

    def product(it, h, e, of_core):
        dst = lax.rem(chip + e, chips) * 2 + of_core
        rows = pl.ds(pl.multiple_of(dst * owned, owned), owned)
        return jnp.dot(link[rows, :], panels[it, h], preferred_element_type=jnp.float32)

    for d in range(1, n_col):
        sums_copy(d).start()

    @pl.loop(0, tile_rows)
    def _(i):
        for j in range(tile_cols):
            slot = slot_ref[i * tile_cols + j]
            tile = adj_ref[jnp.maximum(slot - 1, 0)]
            link[pl.ds(i * edge, edge), j * edge : (j + 1) * edge] = jnp.where(
                slot > 0, tile, jnp.zeros_like(tile)
            )

    total = sums_out[c, :held]
    for d in range(1, n_col):
        sums_copy(d).wait_recv()
        total = total + sums_in[d, :held]
    scale = 1.0 / jnp.maximum(total, 1.0)
    for t in range(held):
        wide = jnp.broadcast_to(scale[t : t + 1], (LANES, edge))
        inverse[t * edge : (t + 1) * edge] = jnp.transpose(wide)

    def share(it, h, ranks):
        place = pl.ds(pl.multiple_of(c * owned, owned), owned)
        panels[it, h, place] = (ranks * inverse[...]).astype(jnp.bfloat16)
        for d in range(1, n_col):
            col_copy(it, h, d).start()

    share(0, 0, prev_ref[:, :LANES])

    for it in range(ITERS):
        for h in range(chunks):
            for d in range(1, n_col):
                col_copy(it, h, d).wait_recv()
            if it == 0 and h + 1 < chunks:
                share(0, h + 1, prev_ref[:, (h + 1) * LANES : (h + 2) * LANES])
            @pl.loop(1, chips + 1, unroll=chips <= 2)
            def _(e):
                place = lax.rem(e, chips)
                pair_out[it, h, place] = product(it, h, place, 1 - core)
                pair_copy(it, h, place).start()

            @pl.loop(1, chips + 1, unroll=chips <= 2)
            def _(e):
                place = lax.rem(e, chips)
                kept[it, h, place] = product(it, h, place, core)

            for e in range(1, chips):
                pair_copy(it, h, e).wait_recv()
                part = kept[it, h, e] + pair_in[it, h, e]
                if it == ITERS - 1:
                    full_out[h, e] = part
                else:
                    half_out[it, h, e] = part.astype(jnp.bfloat16)
                row_copy(it, h, e).start()
            pair_copy(it, h, 0).wait_recv()
            summed = kept[it, h, 0] + pair_in[it, h, 0]
            for e in range(1, chips):
                row_copy(it, h, e).wait_recv()
                if it == ITERS - 1:
                    summed = summed + full_in[h, e]
                else:
                    summed = summed + half_in[it, h, e].astype(jnp.float32)
            lanes = slice(h * LANES, (h + 1) * LANES)
            ranks = DAMPING * summed + restart[:, lanes]
            if it == ITERS - 1:
                out_ref[:, lanes] = ranks
            else:
                share(it + 1, h, ranks)

    for d in range(1, n_col):
        sums_copy(d).wait_send()
    for it in range(ITERS):
        for h in range(chunks):
            for d in range(1, n_col):
                col_copy(it, h, d).wait_send()
            for e in range(chips):
                pair_copy(it, h, e).wait_send()
            for e in range(1, chips):
                row_copy(it, h, e).wait_send()


def on_device(adjacency, tile_row, tile_col, seed_node, teleport_block, previous):
    tiles = adjacency[0, 0]
    rows, cols = tile_row[0, 0], tile_col[0, 0]
    slots, edge = tiles.shape[:2]
    owned, seeds = previous.shape
    n_row, n_col = lax.axis_size("row"), lax.axis_size("col")
    targets, sources = n_row * owned, n_col * owned
    tile_rows, tile_cols = targets // edge, sources // edge
    chunks, chips = seeds // LANES, n_row // 2
    key = jnp.where(rows >= 0, rows * tile_cols + cols, -1)
    places = jnp.arange(tile_rows * tile_cols, dtype=jnp.int32)
    number = jnp.arange(1, slots + 1, dtype=jnp.int32)
    slot_of = jnp.sum(jnp.where(places[:, None] == key[None, :], number[None, :], 0), axis=1)
    vmem = pl.BlockSpec(memory_space=pltpu.VMEM)
    dma = pltpu.SemaphoreType.DMA
    return pl.pallas_call(
        functools.partial(refresh_kernel, n_row, n_col),
        out_shape=jax.ShapeDtypeStruct((owned, seeds), jnp.float32),
        in_specs=[pl.BlockSpec(memory_space=pltpu.SMEM), pl.BlockSpec(memory_space=pl.ANY)] + [vmem] * 4,
        out_specs=vmem,
        scratch_shapes=[
            pltpu.VMEM(tiles.shape, jnp.bfloat16),
            dma,
            pltpu.VMEM((targets, sources), jnp.bfloat16),
            pltpu.VMEM((n_col, 8, edge), jnp.float32),
            pltpu.VMEM((n_col, 8, edge), jnp.float32),
            pltpu.VMEM((owned, LANES), jnp.float32),
            pltpu.VMEM((owned, seeds), jnp.float32),
            pltpu.VMEM((ITERS, chunks, sources, LANES), jnp.bfloat16),
            pltpu.VMEM((ITERS, chunks, chips, owned, LANES), jnp.float32),
            pltpu.VMEM((ITERS, chunks, chips, owned, LANES), jnp.float32),
            pltpu.VMEM((ITERS, chunks, chips, owned, LANES), jnp.float32),
            pltpu.VMEM((ITERS - 1, chunks, chips, owned, LANES), jnp.bfloat16),
            pltpu.VMEM((ITERS - 1, chunks, chips, owned, LANES), jnp.bfloat16),
            pltpu.VMEM((chunks, chips, owned, LANES), jnp.float32),
            pltpu.VMEM((chunks, chips, owned, LANES), jnp.float32),
            dma((n_col,)),
            dma((n_col,)),
            dma((ITERS, chunks, n_col)),
            dma((ITERS, chunks, n_col)),
            dma((ITERS, chunks, chips)),
            dma((ITERS, chunks, chips)),
            dma((ITERS, chunks, chips)),
            dma((ITERS, chunks, chips)),
        ],
        compiler_params=pltpu.CompilerParams(
            collective_id=0, has_side_effects=True, vmem_limit_bytes=56 * 2**20
        ),
    )(slot_of, tiles, cols[None, :], seed_node[None, :], teleport_block[None, :], previous)


def solution(mesh):
    in_specs = (
        P(("groups", "row"), "col", None, None, None),
        P(("groups", "row"), "col", None),
        P(("groups", "row"), "col", None),
        P("groups"),
        P("groups"),
        P(("groups", "row", "col"), None),
    )
    out_specs = P(("groups", "row", "col"), None)
    return jax.shard_map(
        on_device, mesh=mesh, in_specs=in_specs, out_specs=out_specs, check_vma=False
    )
```

time: 62.4 us -> 58.1 us (0.931); the launches traced: 61.2 us -> 57.9 us
  Pallas kernels: 58.3 us -> 54.9 us
    pallas_call x1, Pallas kernels: 58.3 us -> 54.9 us  [on_device(): pl.pallas_call(functools.partial(refresh_kernel, n_row, n_col), out_shape...]
where the time goes in v2:
time: 58.1 us; the launch traced here: 57.9 us
  Pallas kernels  54.9 us (94%)
  local copies, waits for them, and re-layouts  2.34 us (4%)
  other arithmetic  0.61 us (1%)
    pallas_call x1, Pallas kernels, on_device(): pl.pallas_call(functools.partial(refresh_kernel, n_row, n_col), out_shape...  54.9 us
    unnamed x5, local copies, waits for them, and re-layouts  2.34 us

profile of v2, /device:TPU:0, one launch (start us, length us, event | category | flops | bytes accessed | tf_op | source)
XLA Modules:
  0.0 57.9 jit_solution(8275729609830373974)
XLA Ops:
  0.0 0.0 copy-start
  0.0 0.0 copy-start.1
  0.0 0.7 %copy-done = s32[1,1,32]{2,1,0:T(1,128)S(1)} copy-done((s32[1,1,32]{2,1,0:T(1,128)S(1)}, s32[1,1,32]{2,1,0:T(1,128)}, u32[]{:S(2)}) %copy-start) | copy-done | bytes 152
  0.7 0.0 copy-done.1
  0.7 0.6 %select_reduce_fusion.slot_ref = s32[64]{0:T(128)} fusion(s32[32]{0:T(128)S(1)} %iota_add_fusion, s32[32]{0:T(128)S(1)} %fusion), kind=kLoop, calls=%fused_computation | loop fusion | flops 6080 | bytes 512 | tf_op jit(solution)/shard_map/reduce_sum | solution.py:194
  1.3 54.9 %shard_map.64 = f32[256,256]{1,0:T(8,128)} custom-call(s32[64]{0:T(128)} %select_reduce_fusion.slot_ref, bf16[32,128,128]{2,1,0:T(8,128)(2,1)} %bitcast.6, s32[1,32]{1,0:T(1,128)} %bitcast.9, s32[1,256]{1,0:T(1,128)} %bitcast.7, s32[1,256]{1,0:T(1,128)} %bitcast.8, f32[256,256]{1,0:T(8,128)} %prev_ref.1), custom_call_target="tpu_custom_call" | custom-call | tf_op jit(solution)/shard_map/pallas_call | solution.py:197
  56.2 1.7 %copy.8 = f32[256,256]{1,0:T(8,128)} copy(f32[256,256]{1,0:T(8,128)} %shard_map.64) | data formatting | bytes 524288
  (2 shorter events, 0.0 us)
Async XLA Ops:
  0.0 0.7 %copy-start = (s32[1,1,32]{2,1,0:T(1,128)S(1)}, s32[1,1,32]{2,1,0:T(1,128)}, u32[]{:S(2)}) copy-start(s32[1,1,32]{2,1,0:T(1,128)} %param.8) | copy-start | bytes 388
  0.0 0.7 %copy-start.1 = (s32[1,1,32]{2,1,0:T(1,128)S(1)}, s32[1,1,32]{2,1,0:T(1,128)}, u32[]{:S(2)}) copy-start(s32[1,1,32]{2,1,0:T(1,128)} %param.7) | copy-start | bytes 388

commit v3 on v2

--- a/solution.py
+++ b/solution.py
@@ -131,8 +131,6 @@
         for h in range(chunks):
             for d in range(1, n_col):
                 col_copy(it, h, d).wait_recv()
-            if it == 0 and h + 1 < chunks:
-                share(0, h + 1, prev_ref[:, (h + 1) * LANES : (h + 2) * LANES])
             @pl.loop(1, chips + 1, unroll=chips <= 2)
             def _(e):
                 place = lax.rem(e, chips)
@@ -144,6 +142,8 @@
                 place = lax.rem(e, chips)
                 kept[it, h, place] = product(it, h, place, core)
 
+            if it == 0 and h + 1 < chunks:
+                share(0, h + 1, prev_ref[:, (h + 1) * LANES : (h + 2) * LANES])
             for e in range(1, chips):
                 pair_copy(it, h, e).wait_recv()
                 part = kept[it, h, e] + pair_in[it, h, e]

time: 58.1 us -> 57.4 us (0.988)
  Pallas kernels: 54.9 us -> 54.2 us
    pallas_call x1, Pallas kernels: 54.9 us -> 54.2 us  [on_device(): pl.pallas_call(functools.partial(refresh_kernel, n_row, n_col), out_shape...]
where the time goes in v3:
time: 57.4 us; the launch traced here: 57.2 us
  Pallas kernels  54.2 us (94%)
  local copies, waits for them, and re-layouts  2.34 us (4%)
  other arithmetic  0.61 us (1%)
    pallas_call x1, Pallas kernels, on_device(): pl.pallas_call(functools.partial(refresh_kernel, n_row, n_col), out_shape...  54.2 us
    unnamed x5, local copies, waits for them, and re-layouts  2.34 us

profile of v3, /device:TPU:0, one launch (start us, length us, event | category | flops | bytes accessed | tf_op | source)
XLA Modules:
  0.0 57.2 jit_solution(10604870463348596503)
XLA Ops:
  0.0 0.0 copy-start
  0.0 0.0 copy-start.1
  0.0 0.7 %copy-done = s32[1,1,32]{2,1,0:T(1,128)S(1)} copy-done((s32[1,1,32]{2,1,0:T(1,128)S(1)}, s32[1,1,32]{2,1,0:T(1,128)}, u32[]{:S(2)}) %copy-start) | copy-done | bytes 152
  0.7 0.0 copy-done.1
  0.7 0.6 %select_reduce_fusion.slot_ref = s32[64]{0:T(128)} fusion(s32[32]{0:T(128)S(1)} %iota_add_fusion, s32[32]{0:T(128)S(1)} %fusion), kind=kLoop, calls=%fused_computation | loop fusion | flops 6080 | bytes 512 | tf_op jit(solution)/shard_map/reduce_sum | solution.py:194
  1.3 54.2 %shard_map.64 = f32[256,256]{1,0:T(8,128)} custom-call(s32[64]{0:T(128)} %select_reduce_fusion.slot_ref, bf16[32,128,128]{2,1,0:T(8,128)(2,1)} %bitcast.6, s32[1,32]{1,0:T(1,128)} %bitcast.9, s32[1,256]{1,0:T(1,128)} %bitcast.7, s32[1,256]{1,0:T(1,128)} %bitcast.8, f32[256,256]{1,0:T(8,128)} %prev_ref.1), custom_call_target="tpu_custom_call" | custom-call | tf_op jit(solution)/shard_map/pallas_call | solution.py:197
  55.5 1.7 %copy.8 = f32[256,256]{1,0:T(8,128)} copy(f32[256,256]{1,0:T(8,128)} %shard_map.64) | data formatting | bytes 524288
  (2 shorter events, 0.0 us)
Async XLA Ops:
  0.0 0.7 %copy-start = (s32[1,1,32]{2,1,0:T(1,128)S(1)}, s32[1,1,32]{2,1,0:T(1,128)}, u32[]{:S(2)}) copy-start(s32[1,1,32]{2,1,0:T(1,128)} %param.8) | copy-start | bytes 388
  0.0 0.7 %copy-start.1 = (s32[1,1,32]{2,1,0:T(1,128)S(1)}, s32[1,1,32]{2,1,0:T(1,128)}, u32[]{:S(2)}) copy-start(s32[1,1,32]{2,1,0:T(1,128)} %param.7) | copy-start | bytes 388
